TPU v7x, 32 devices: a whole 2x2x4 slice. The times are simulated.
32 devices in a mesh: col: 4 (over y, x), row: 8 (over z, core).
Axes of the slice: x: 2, y: 2, z: 4, core: 2. Of those that a mesh axis runs over, the one named last changes fastest.
Arguments:
- density: float32 [8, 512, 1024], P(None, 'row', 'col'), may hold values from 1 to 2
- velocity: float32 [3, 8, 512, 1024], P(None, None, 'row', 'col'), may hold values from -0.3 to 0.3
- pressure: float32 [8, 512, 1024], P(None, 'row', 'col'), may hold values from 1 to 2
Outputs:
- density_out: float32 [8, 512, 1024], P(None, 'row', 'col')
- velocity_out: float32 [3, 8, 512, 1024], P(None, None, 'row', 'col')
- pressure_out: float32 [8, 512, 1024], P(None, 'row', 'col')
All inputs are finite; a program needn't handle non-finite values.
Results may differ from a plain program's by a relative error of at most 0.00002.
Values sent between devices are 32-bit elements; how exact they have to be, the bound alone decides.
A program may use at most 128 MiB of HBM per device.

v0:
```python
import functools

import jax
import jax.numpy as jnp
from jax import lax
from jax.experimental import pallas as pl
from jax.experimental.pallas import tpu as pltpu
from jax.sharding import PartitionSpec as P

NU = 0.15
PER_R = 1.0 / 1.2
SIGMA = 1.68**0.5
GUESS = (7.0 / 6.0) ** 0.5
UNROLL = 8
LANES = 128
EDGE = 4


def recip(x):
    return pltpu.reciprocal(x, approx=True)


def clip(x, lo, hi):
    return jnp.maximum(lo, jnp.minimum(x, hi))


def riemann(left, right):
    r_l, u_l, p_l = left
    r_r, u_r, p_r = right
    dp = p_r - p_l
    du = u_r - u_l
    j_l = lax.rsqrt(p_l * r_l)
    j_r = lax.rsqrt(p_r * r_r)
    rise = (j_r * dp - GUESS * du) * recip(j_l + j_r)
    a_l = (7.0 / 6.0) * p_l
    a_r = (1.0 / 6.0) * p_r + p_l
    for _ in range(2):
        j_l = lax.rsqrt(r_l * (a_l + rise))
        j_r = lax.rsqrt(r_r * (a_r + rise))
        rise = (j_r * dp - du) * recip(j_l + j_r)
    return p_l + rise, u_l - rise * j_l


EMPTY = (None,) * 9


def step(carry, new, conserved, emit):
    a3, a2, a1, h, bounds, face, star, lag, flux = carry
    nxt = [a2, a1, new] + [None] * 6
    if a3 is None:
        return tuple(nxt)
    lo = [jnp.minimum(x, y) for x, y in zip(a2, a1)]
    hi = [jnp.maximum(x, y) for x, y in zip(a2, a1)]
    h_new = tuple(
        clip((x2 + x1) * (7.0 / 12.0) - (x3 + x0) * (1.0 / 12.0), l, u)
        for x3, x2, x1, x0, l, u in zip(a3, a2, a1, new, lo, hi)
    )
    nxt[3] = h_new
    nxt[4] = tuple(lo + hi)
    if h is None:
        return tuple(nxt)
    sg = a2[2] * lax.rsqrt(a2[2] * a2[0]) * SIGMA
    m = 1.0 - sg
    b = sg * m
    e = sg + (b + b)
    base = [e * x - b * (am + ap) for x, am, ap in zip(a2, h, h_new)]
    nxt[5] = tuple(clip(x + m * ap, l, u) for x, ap, l, u in zip(base, h_new, lo, hi))
    if face is None:
        return tuple(nxt)
    left = [clip(x + m * am, l, u) for x, am, l, u in zip(base, h, bounds[:3], bounds[3:])]
    p_star, u_star = riemann(face, left)
    p_hat = 1.2 * p_star
    work = (p_hat + p_hat) * u_star
    nxt[6] = (u_star, p_hat, work)
    if star is None:
        return tuple(nxt)
    mass, m_n, m_s, m_t, en = conserved()
    m_n = m_n - p_hat + star[1]
    en = en - work + star[2]
    width = 1.0 + (u_star - star[0])
    cell = (mass, m_n, m_s, m_t, en)
    nxt[7] = cell + (width,)
    if lag is None:
        return tuple(nxt)
    ahead = star[0] > 0.0
    swept = star[0] * recip(jnp.where(ahead, lag[5], width))
    g = tuple(swept * jnp.where(ahead, x, y) for x, y in zip(lag[:5], cell))
    nxt[8] = g
    if flux is None:
        return tuple(nxt)
    emit(*[x - y + z for x, y, z in zip(lag[:5], g, flux)])
    return tuple(nxt)


def conserved_of(r, u, v, w, p):
    m_u, m_v, m_w = r * u, r * v, r * w
    return r, m_u, m_v, m_w, 6.0 * p + (m_u * u + m_v * v + m_w * w)


def after_y_values(mass, m_y, m_x, m_z, en):
    r = recip(mass)
    pi = (en - (m_x * m_x + m_y * m_y + m_z * m_z) * r) * (1.0 / 6.0)
    return mass, m_z * r, pi, m_x, m_y, en


def y_kernel(axes, planes, ny, halves, d_in, v_in, p_in, t_out, yb, ek, hr, ab, ho, send, recv):
    nrow, ncol = axes
    row, col = lax.axis_index("row"), lax.axis_index("col")
    up, dn = lax.rem(row + nrow - 1, nrow), lax.rem(row + 1, nrow)
    lf, rt = lax.rem(col + ncol - 1, ncol), lax.rem(col + 1, ncol)

    def at(r, c):
        return {"row": r, "col": c}

    around = [(up, col), (dn, col), (row, lf), (row, rt), (up, lf), (up, rt), (dn, lf), (dn, rt)]
    barrier = pltpu.get_barrier_semaphore()
    for r, c in around:
        pl.semaphore_signal(
            barrier, inc=1, device_id=at(r, c), device_id_type=pl.DeviceIdType.MESH
        )

    rows = planes * ny
    lane = lax.broadcasted_iota(jnp.int32, (8, LANES), 1)
    scales = (1.2, NU, NU, NU, NU * NU)
    refs = (
        d_in,
        v_in.at[pl.ds(0, rows)],
        v_in.at[pl.ds(rows, rows)],
        v_in.at[pl.ds(2 * rows, rows)],
        p_in,
    )

    def pack(b, _):
        y0 = pl.multiple_of(b * 8, 8)
        for f in range(5):
            acc = jnp.ones((8, LANES), jnp.float32)
            for p in range(planes):
                src = pl.ds(pl.multiple_of(p * ny + y0, 8), 8)
                last = refs[f][src, pl.ds((halves - 1) * LANES, LANES)]
                fst = refs[f][src, pl.ds(0, LANES)]
                last = pltpu.roll(last, EDGE * p + EDGE, 1)
                fst = pltpu.roll(fst, 32 + EDGE * p, 1)
                acc = jnp.where(lane // EDGE == p, last, acc)
                acc = jnp.where(lane // EDGE == 8 + p, fst, acc)
            ek[f, pl.ds(y0, 8), :] = acc * scales[f]
        return 0

    def spread(y, _):
        for f in range(5):
            for h in range(halves):
                x = ab[f, h, pl.ds(y, planes, stride=ny), :]
                yb[f, h, y + EDGE] = x * scales[f]
        return 0

    def place(b, _):
        r0 = pl.ds(pl.multiple_of(b * 8, 8), 8)
        for f in range(5):
            for h in range(halves):
                ab[f, h, r0, :] = refs[f][r0, pl.ds(h * LANES, LANES)]
        return 0

    lax.fori_loop(0, rows // 8, place, 0, unroll=4)
    lax.fori_loop(0, ny, spread, 0, unroll=4)
    lax.fori_loop(0, ny // 8, pack, 0)

    pl.semaphore_wait(barrier, len(around))

    def rows_of(start, size):
        return yb.at[:, :, pl.ds(start, size)]

    sends = [
        (rows_of(EDGE, EDGE), rows_of(ny + EDGE, EDGE), (up, col)),
        (rows_of(ny, EDGE), rows_of(0, EDGE), (dn, col)),
        (ek, hr.at[0, :, pl.ds(8, ny)], (row, rt)),
        (ek, hr.at[1, :, pl.ds(8, ny)], (row, lf)),
        (ek.at[:, pl.ds(ny - 8, 8)], hr.at[0, :, pl.ds(0, 8)], (dn, rt)),
        (ek.at[:, pl.ds(ny - 8, 8)], hr.at[1, :, pl.ds(0, 8)], (dn, lf)),
        (ek.at[:, pl.ds(0, 8)], hr.at[0, :, pl.ds(ny + 8, 8)], (up, rt)),
        (ek.at[:, pl.ds(0, 8)], hr.at[1, :, pl.ds(ny + 8, 8)], (up, lf)),
    ]
    copies = []
    for k, (src, dst, who) in enumerate(sends):
        copy = pltpu.make_async_remote_copy(
            src_ref=src,
            dst_ref=dst,
            send_sem=send.at[k],
            recv_sem=recv.at[k],
            device_id=at(*who),
            device_id_type=pl.DeviceIdType.MESH,
        )
        copy.start()
        copies.append(copy)

    def y_step(carry, c, h):
        def load(f, i):
            return yb[f, h, i + EDGE]

        def cons():
            r, x, y, z, p = (load(f, c - 3) for f in range(5))
            return conserved_of(r, y, x, z, p)

        def emit(*values):
            for f, x in enumerate(after_y_values(*values)):
                ab[f, h, pl.ds(c - EDGE, planes, stride=ny), :] = x

        return step(carry, tuple(load(f, c) for f in (0, 2, 4)), cons, emit)

    def y_steps(carries, start, count):
        for k in range(count):
            carries = tuple(y_step(carries[h], start + k, h) for h in range(halves))
        return carries

    carries = y_steps((EMPTY,) * halves, 0, 8)
    carries = lax.fori_loop(
        0,
        (ny - 8) // UNROLL,
        lambda i, cr: y_steps(cr, 8 + i * UNROLL, UNROLL),
        carries,
    )
    for copy in copies:
        copy.wait()
    y_steps(carries, ny, EDGE)
    y_steps((EMPTY,) * halves, -EDGE, 12)

    def z_load(f, c):
        s = pl.ds(8 + c, 8, stride=ny // 8)
        return jnp.where(lane < 32, hr[0, f, s, :], hr[1, f, s, :])

    carry = EMPTY
    for c in range(-EDGE, ny // 8 + EDGE):

        def cons(c=c):
            r, x, y, z, p = (z_load(f, c - 3) for f in range(5))
            return conserved_of(r, y, x, z, p)

        def emit(*values, c=c):
            for f, x in enumerate(after_y_values(*values)):
                ho[f, pl.ds(c - EDGE, 8, stride=ny // 8), :] = x

        carry = step(carry, tuple(z_load(f, c) for f in (0, 2, 4)), cons, emit)

    pitch = LANES + 16
    groups = rows // LANES
    for f in range(6):
        for g in range(groups):
            tiles = [ab[f, h, pl.ds(g * LANES, LANES), :].T for h in range(halves)]
            for h in range(halves):
                k = (g * halves + h) * pitch
                t_out[f, pl.ds(k + 8, LANES), :] = tiles[h]
                if h > 0:
                    t_out[f, pl.ds(k + EDGE, EDGE), :] = tiles[h - 1][LANES - EDGE :]
                if h + 1 < halves:
                    t_out[f, pl.ds(k + 8 + LANES, EDGE), :] = tiles[h + 1][:EDGE]
        edge = ho[f]
        both = jnp.concatenate([edge, pltpu.roll(edge, LANES - EDGE, 1)], axis=0).T
        for g in range(groups):
            k = g * halves * pitch
            t_out[f, pl.ds(k + EDGE, EDGE), :] = both[8 * g : 8 * g + EDGE]
            k = (g * halves + halves - 1) * pitch
            t_out[f, pl.ds(k + 8 + LANES, EDGE), :] = both[32 + 8 * g : 32 + 8 * g + EDGE]


def z_kernel(planes, ny, halves, t_in, d_out, v_out, p_out, zb):
    rows = planes * ny
    groups = rows // LANES
    pitch = LANES + 16
    out_pitch = LANES + 8
    blocks = groups * halves

    def load(f, c):
        return t_in[f, pl.ds(c + 8, blocks, stride=pitch), :]

    def z_step(carry, c):
        def cons():
            r, u, _, m_x, m_y, en = (load(f, c - 3) for f in range(6))
            return r, r * u, m_x, m_y, en

        def emit(mass, m_z, m_x, m_y, en):
            r = recip(mass)
            p = (en - (m_x * m_x + m_y * m_y + m_z * m_z) * r) * (1.0 / (6.0 * NU * NU))
            r = r * (1.0 / NU)
            for f, x in enumerate((mass * PER_R, m_x * r, m_y * r, m_z * r, p)):
                zb[f, pl.ds(c - EDGE, blocks, stride=out_pitch), :] = x

        return step(carry, tuple(load(f, c) for f in range(3)), cons, emit)

    carry = EMPTY
    for c in range(-EDGE, EDGE):
        carry = z_step(carry, c)

    def turn(i, carry):
        for k in range(UNROLL):
            carry = z_step(carry, EDGE + i * UNROLL + k)
        return carry

    lax.fori_loop(0, LANES // UNROLL, turn, carry)

    outs = [
        d_out,
        v_out.at[pl.ds(0, rows)],
        v_out.at[pl.ds(rows, rows)],
        v_out.at[pl.ds(2 * rows, rows)],
        p_out,
    ]
    for f in range(5):
        for g in range(groups):
            for h in range(halves):
                k = (g * halves + h) * out_pitch
                outs[f][pl.ds(g * LANES, LANES), pl.ds(h * LANES, LANES)] = zb[
                    f, pl.ds(k, LANES), :
                ].T


def on_device(axes, density, velocity, pressure):
    planes, ny, nz = density.shape
    rows, halves = planes * ny, nz // LANES
    pitch = LANES + 16
    blocks = rows // LANES * halves
    f32 = jnp.float32
    vmem = pl.BlockSpec(memory_space=pltpu.VMEM)
    turned = pl.pallas_call(
        functools.partial(y_kernel, axes, planes, ny, halves),
        out_shape=jax.ShapeDtypeStruct((6, blocks * pitch, LANES), f32),
        in_specs=[vmem] * 3,
        out_specs=vmem,
        scratch_shapes=[
            pltpu.VMEM((5, halves, ny + 2 * EDGE, planes, LANES), f32),
            pltpu.VMEM((5, ny, LANES), f32),
            pltpu.VMEM((2, 5, ny + 16, LANES), f32),
            pltpu.VMEM((6, halves, rows, LANES), f32),
            pltpu.VMEM((6, ny, LANES), f32),
            pltpu.SemaphoreType.DMA((8,)),
            pltpu.SemaphoreType.DMA((8,)),
        ],
        compiler_params=pltpu.CompilerParams(
            collective_id=0, has_side_effects=True, vmem_limit_bytes=40 * 2**20
        ),
    )(density.reshape(rows, nz), velocity.reshape(3 * rows, nz), pressure.reshape(rows, nz))
    d, v, p = pl.pallas_call(
        functools.partial(z_kernel, planes, ny, halves),
        out_shape=[
            jax.ShapeDtypeStruct((rows, nz), f32),
            jax.ShapeDtypeStruct((3 * rows, nz), f32),
            jax.ShapeDtypeStruct((rows, nz), f32),
        ],
        in_specs=[vmem],
        out_specs=[vmem] * 3,
        scratch_shapes=[pltpu.VMEM((5, blocks * (LANES + 8), LANES), f32)],
        compiler_params=pltpu.CompilerParams(vmem_limit_bytes=40 * 2**20),
    )(turned)
    return d.reshape(density.shape), v.reshape(velocity.shape), p.reshape(density.shape)


def solution(mesh):
    field = P(None, "row", "col")
    vector = P(None, None, "row", "col")
    axes = (mesh.shape["row"], mesh.shape["col"])
    return jax.shard_map(
        functools.partial(on_device, axes),
        mesh=mesh,
        in_specs=(field, vector, field),
        out_specs=(field, vector, field),
        check_vma=False,
    )
```

profile of v0, /device:TPU:1, one launch (start us, length us, event | category | flops | bytes accessed | tf_op | source)
XLA Modules:
  0.0 28.6 jit_solution(14345326050163123561)
XLA Ops:
  0.6 0.0 copy-start
  0.6 1.4 %copy-done = f32[3,8,64,256]{3,2,1,0:T(8,128)S(1)} copy-done((f32[3,8,64,256]{3,2,1,0:T(8,128)S(1)}, f32[3,8,64,256]{3,2,1,0:T(8,128)}, u32[]{:S(2)}) %copy-start) | copy-done | bytes 1572888
  2.0 0.0 copy-start.1
  2.0 1.0 %copy-done.1 = f32[8,64,256]{2,1,0:T(8,128)S(1)} copy-done((f32[8,64,256]{2,1,0:T(8,128)S(1)}, f32[8,64,256]{2,1,0:T(8,128)}, u32[]{:S(2)}) %copy-start.1) | copy-done | bytes 524312
  3.1 0.0 copy-start.2
  3.1 1.0 %copy-done.2 = f32[8,64,256]{2,1,0:T(8,128)S(1)} copy-done((f32[8,64,256]{2,1,0:T(8,128)S(1)}, f32[8,64,256]{2,1,0:T(8,128)}, u32[]{:S(2)}) %copy-start.2) | copy-done | bytes 524312
  4.1 18.1 %shard_map.58.t_in = f32[6,1152,128]{2,1,0:T(8,128)S(1)} custom-call(f32[512,256]{1,0:T(8,128)S(1)} %bitcast.7, f32[1536,256]{1,0:T(8,128)S(1)} %bitcast.6, f32[512,256]{1,0:T(8,128)S(1)} %bitcast.8), custom_call_target="tpu_custom_call" | custom-call | tf_op jit(solution)/shard_map/pallas_call | solution.py:321
  22.2 6.3 %shard_map.59 = (f32[512,256]{1,0:T(8,128)}, f32[1536,256]{1,0:T(8,128)}, f32[512,256]{1,0:T(8,128)}) custom-call(f32[6,1152,128]{2,1,0:T(8,128)S(1)} %shard_map.58.t_in), custom_call_target="tpu_custom_call" | custom-call | tf_op jit(solution)/shard_map/pallas_call | solution.py:339
Async XLA Ops:
  0.6 1.4 %copy-start = (f32[3,8,64,256]{3,2,1,0:T(8,128)S(1)}, f32[3,8,64,256]{3,2,1,0:T(8,128)}, u32[]{:S(2)}) copy-start(f32[3,8,64,256]{3,2,1,0:T(8,128)} %param.4) | copy-start | bytes 4718596
  2.0 1.0 %copy-start.1 = (f32[8,64,256]{2,1,0:T(8,128)S(1)}, f32[8,64,256]{2,1,0:T(8,128)}, u32[]{:S(2)}) copy-start(f32[8,64,256]{2,1,0:T(8,128)} %param.3) | copy-start | bytes 1572868
  3.1 1.0 %copy-start.2 = (f32[8,64,256]{2,1,0:T(8,128)S(1)}, f32[8,64,256]{2,1,0:T(8,128)}, u32[]{:S(2)}) copy-start(f32[8,64,256]{2,1,0:T(8,128)} %param.5) | copy-start | bytes 1572868
where the time goes:
time: 28.8 us; the launch traced here: 28.6 us
  Pallas kernels  24.5 us (85%)
  local copies, waits for them, and re-layouts  3.48 us (12%)
  between operations  0.65 us (2%)
    pallas_call x1, Pallas kernels, on_device(): pl.pallas_call(functools.partial(y_kernel, axes, planes, ny, halves), out...  18.1 us
    pallas_call x1, Pallas kernels, on_device(): pl.pallas_call(functools.partial(z_kernel, planes, ny, halves), out_shape...  6.34 us
    unnamed x6, local copies, waits for them, and re-layouts  3.48 us

commit v1 on v0

--- a/solution.py
+++ b/solution.py
@@ -103,7 +103,10 @@
     return mass, m_z * r, pi, m_x, m_y, en
 
 
-def y_kernel(axes, planes, ny, halves, d_in, v_in, p_in, t_out, yb, ek, hr, ab, ho, send, recv):
+def y_kernel(
+    axes, planes, ny, halves, d_in, v_in, p_in, t_out,
+    xin, yb, ek, pk, pr, cr, hr, ab, ho, load_sem, send, recv,
+):
     nrow, ncol = axes
     row, col = lax.axis_index("row"), lax.axis_index("col")
     up, dn = lax.rem(row + nrow - 1, nrow), lax.rem(row + 1, nrow)
@@ -129,6 +132,21 @@
         v_in.at[pl.ds(2 * rows, rows)],
         p_in,
     )
+    loads = []
+    for f in range(5):
+        for h in range(halves):
+            copy = pltpu.make_async_copy(
+                refs[f].at[:, pl.ds(h * LANES, LANES)], xin.at[f, h], load_sem.at[f, h]
+            )
+            copy.start()
+            loads.append(copy)
+
+    def spread(y, _):
+        for f in range(5):
+            for h in range(halves):
+                x = xin[f, h, pl.ds(y, planes, stride=ny), :]
+                yb[f, h, y + EDGE] = x * scales[f]
+        return 0
 
     def pack(b, _):
         y0 = pl.multiple_of(b * 8, 8)
@@ -136,50 +154,16 @@
             acc = jnp.ones((8, LANES), jnp.float32)
             for p in range(planes):
                 src = pl.ds(pl.multiple_of(p * ny + y0, 8), 8)
-                last = refs[f][src, pl.ds((halves - 1) * LANES, LANES)]
-                fst = refs[f][src, pl.ds(0, LANES)]
-                last = pltpu.roll(last, EDGE * p + EDGE, 1)
-                fst = pltpu.roll(fst, 32 + EDGE * p, 1)
+                last = pltpu.roll(xin[f, halves - 1, src, :], EDGE * p + EDGE, 1)
+                fst = pltpu.roll(xin[f, 0, src, :], 32 + EDGE * p, 1)
                 acc = jnp.where(lane // EDGE == p, last, acc)
                 acc = jnp.where(lane // EDGE == 8 + p, fst, acc)
             ek[f, pl.ds(y0, 8), :] = acc * scales[f]
         return 0
 
-    def spread(y, _):
-        for f in range(5):
-            for h in range(halves):
-                x = ab[f, h, pl.ds(y, planes, stride=ny), :]
-                yb[f, h, y + EDGE] = x * scales[f]
-        return 0
-
-    def place(b, _):
-        r0 = pl.ds(pl.multiple_of(b * 8, 8), 8)
-        for f in range(5):
-            for h in range(halves):
-                ab[f, h, r0, :] = refs[f][r0, pl.ds(h * LANES, LANES)]
-        return 0
-
-    lax.fori_loop(0, rows // 8, place, 0, unroll=4)
-    lax.fori_loop(0, ny, spread, 0, unroll=4)
-    lax.fori_loop(0, ny // 8, pack, 0)
-
-    pl.semaphore_wait(barrier, len(around))
-
-    def rows_of(start, size):
-        return yb.at[:, :, pl.ds(start, size)]
-
-    sends = [
-        (rows_of(EDGE, EDGE), rows_of(ny + EDGE, EDGE), (up, col)),
-        (rows_of(ny, EDGE), rows_of(0, EDGE), (dn, col)),
-        (ek, hr.at[0, :, pl.ds(8, ny)], (row, rt)),
-        (ek, hr.at[1, :, pl.ds(8, ny)], (row, lf)),
-        (ek.at[:, pl.ds(ny - 8, 8)], hr.at[0, :, pl.ds(0, 8)], (dn, rt)),
-        (ek.at[:, pl.ds(ny - 8, 8)], hr.at[1, :, pl.ds(0, 8)], (dn, lf)),
-        (ek.at[:, pl.ds(0, 8)], hr.at[0, :, pl.ds(ny + 8, 8)], (up, rt)),
-        (ek.at[:, pl.ds(0, 8)], hr.at[1, :, pl.ds(ny + 8, 8)], (up, lf)),
-    ]
     copies = []
-    for k, (src, dst, who) in enumerate(sends):
+
+    def remote(k, src, dst, who):
         copy = pltpu.make_async_remote_copy(
             src_ref=src,
             dst_ref=dst,
@@ -191,6 +175,38 @@
         copy.start()
         copies.append(copy)
 
+    def rows_of(start, size):
+        return yb.at[:, :, pl.ds(start, size)]
+
+    for copy in loads:
+        copy.wait()
+    for y in (*range(EDGE), *range(ny - EDGE, ny)):
+        spread(y, 0)
+    pl.semaphore_wait(barrier, len(around))
+    remote(0, rows_of(EDGE, EDGE), rows_of(ny + EDGE, EDGE), (up, col))
+    remote(1, rows_of(ny, EDGE), rows_of(0, EDGE), (dn, col))
+
+    lax.fori_loop(0, ny // 8, pack, 0)
+    fold = LANES // 32
+    part = ny // fold
+    for f in range(5):
+        for b in range(part // 8):
+            for side in range(2):
+                acc = None
+                for q in range(fold):
+                    x = ek[f, pl.ds(q * part + b * 8, 8), :]
+                    turn = (32 * (q - side)) % LANES
+                    x = pltpu.roll(x, turn, 1) if turn else x
+                    acc = x if acc is None else jnp.where(lane // 32 == q, x, acc)
+                pk[side, f, pl.ds(b * 8, 8), :] = acc
+    remote(2, pk.at[0], pr.at[0], (row, rt))
+    remote(3, pk.at[1], pr.at[1], (row, lf))
+    remote(4, ek.at[:, pl.ds(ny - 8, 8)], cr.at[0, 0], (dn, rt))
+    remote(5, ek.at[:, pl.ds(ny - 8, 8)], cr.at[1, 0], (dn, lf))
+    remote(6, ek.at[:, pl.ds(0, 8)], cr.at[0, 1], (up, rt))
+    remote(7, ek.at[:, pl.ds(0, 8)], cr.at[1, 1], (up, lf))
+    lax.fori_loop(EDGE, ny - EDGE, spread, 0, unroll=4)
+
     def y_step(carry, c, h):
         def load(f, i):
             return yb[f, h, i + EDGE]
@@ -217,14 +233,26 @@
         lambda i, cr: y_steps(cr, 8 + i * UNROLL, UNROLL),
         carries,
     )
-    for copy in copies:
+    for copy in copies[:2]:
         copy.wait()
     y_steps(carries, ny, EDGE)
     y_steps((EMPTY,) * halves, -EDGE, 12)
 
+    for copy in copies[2:]:
+        copy.wait()
+    for f in range(5):
+        for end, start in ((0, 0), (1, ny + 8)):
+            hr[f, pl.ds(start, 8), :] = jnp.where(lane < 32, cr[0, end, f], cr[1, end, f])
+        for b in range(part // 8):
+            for q in range(fold):
+                x = [pr[side, f, pl.ds(b * 8, 8), :] for side in range(2)]
+                for side in range(2):
+                    turn = (32 * (side - q)) % LANES
+                    x[side] = pltpu.roll(x[side], turn, 1) if turn else x[side]
+                hr[f, pl.ds(8 + q * part + b * 8, 8), :] = jnp.where(lane < 32, *x)
+
     def z_load(f, c):
-        s = pl.ds(8 + c, 8, stride=ny // 8)
-        return jnp.where(lane < 32, hr[0, f, s, :], hr[1, f, s, :])
+        return hr[f, pl.ds(8 + c, 8, stride=ny // 8), :]
 
     carry = EMPTY
     for c in range(-EDGE, ny // 8 + EDGE):
@@ -321,21 +349,31 @@
     turned = pl.pallas_call(
         functools.partial(y_kernel, axes, planes, ny, halves),
         out_shape=jax.ShapeDtypeStruct((6, blocks * pitch, LANES), f32),
-        in_specs=[vmem] * 3,
+        in_specs=[pl.BlockSpec(memory_space=pltpu.HBM)] * 3,
         out_specs=vmem,
         scratch_shapes=[
+            pltpu.VMEM((5, halves, rows, LANES), f32),
             pltpu.VMEM((5, halves, ny + 2 * EDGE, planes, LANES), f32),
             pltpu.VMEM((5, ny, LANES), f32),
-            pltpu.VMEM((2, 5, ny + 16, LANES), f32),
+            pltpu.VMEM((2, 5, ny // (LANES // 32), LANES), f32),
+            pltpu.VMEM((2, 5, ny // (LANES // 32), LANES), f32),
+            pltpu.VMEM((2, 2, 5, 8, LANES), f32),
+            pltpu.VMEM((5, ny + 16, LANES), f32),
             pltpu.VMEM((6, halves, rows, LANES), f32),
             pltpu.VMEM((6, ny, LANES), f32),
+            pltpu.SemaphoreType.DMA((5, halves)),
             pltpu.SemaphoreType.DMA((8,)),
             pltpu.SemaphoreType.DMA((8,)),
         ],
         compiler_params=pltpu.CompilerParams(
             collective_id=0, has_side_effects=True, vmem_limit_bytes=40 * 2**20
         ),
-    )(density.reshape(rows, nz), velocity.reshape(3 * rows, nz), pressure.reshape(rows, nz))
+    )(
+        *[
+            pltpu.with_memory_space_constraint(x.reshape(-1, nz), pltpu.HBM)
+            for x in (density, velocity, pressure)
+        ]
+    )
     d, v, p = pl.pallas_call(
         functools.partial(z_kernel, planes, ny, halves),
         out_shape=[

time: 28.8 us -> 24.5 us (0.85)
  the two profiles are of different devices: /device:TPU:1 before, /device:TPU:0 now
where the time goes in v1:
time: 24.5 us; the launch traced here: 24.4 us
  Pallas kernels  23.7 us (97%)
  between operations  0.64 us (3%)
    pallas_call x1, Pallas kernels, on_device(): pl.pallas_call(functools.partial(y_kernel, axes, planes, ny, halves), out...  17.4 us
    pallas_call x1, Pallas kernels, on_device(): pl.pallas_call(functools.partial(z_kernel, planes, ny, halves), out_shape...  6.34 us

profile of v1, /device:TPU:0, one launch (start us, length us, event | category | flops | bytes accessed | tf_op | source)
XLA Modules:
  0.0 24.4 jit_solution(4861725859997221463)
XLA Ops:
  0.6 17.4 %shard_map.58.t_in = f32[6,1152,128]{2,1,0:T(8,128)S(1)} custom-call(f32[512,256]{1,0:T(8,128)} %bitcast.7, f32[1536,256]{1,0:T(8,128)} %bitcast.6, f32[512,256]{1,0:T(8,128)} %bitcast.8), custom_call_target="tpu_custom_call" | custom-call | tf_op jit(solution)/shard_map/pallas_call | solution.py:349
  18.0 6.3 %shard_map.59 = (f32[512,256]{1,0:T(8,128)}, f32[1536,256]{1,0:T(8,128)}, f32[512,256]{1,0:T(8,128)}) custom-call(f32[6,1152,128]{2,1,0:T(8,128)S(1)} %shard_map.58.t_in), custom_call_target="tpu_custom_call" | custom-call | tf_op jit(solution)/shard_map/pallas_call | solution.py:377

commit v2 on v1

--- a/solution.py
+++ b/solution.py
@@ -12,6 +12,7 @@
 SIGMA = 1.68**0.5
 GUESS = (7.0 / 6.0) ** 0.5
 UNROLL = 8
+UNROLL_Z = 32
 LANES = 128
 EDGE = 4
 
@@ -124,13 +125,13 @@
 
     rows = planes * ny
     lane = lax.broadcasted_iota(jnp.int32, (8, LANES), 1)
-    scales = (1.2, NU, NU, NU, NU * NU)
+    scales = (1.2, NU, NU * NU, NU, NU)
     refs = (
         d_in,
+        v_in.at[pl.ds(rows, rows)],
+        p_in,
         v_in.at[pl.ds(0, rows)],
-        v_in.at[pl.ds(rows, rows)],
         v_in.at[pl.ds(2 * rows, rows)],
-        p_in,
     )
     loads = []
     for f in range(5):
@@ -154,10 +155,9 @@
             acc = jnp.ones((8, LANES), jnp.float32)
             for p in range(planes):
                 src = pl.ds(pl.multiple_of(p * ny + y0, 8), 8)
-                last = pltpu.roll(xin[f, halves - 1, src, :], EDGE * p + EDGE, 1)
-                fst = pltpu.roll(xin[f, 0, src, :], 32 + EDGE * p, 1)
-                acc = jnp.where(lane // EDGE == p, last, acc)
-                acc = jnp.where(lane // EDGE == 8 + p, fst, acc)
+                x = jnp.where(lane < EDGE, xin[f, 0, src, :], xin[f, halves - 1, src, :])
+                x = pltpu.roll(x, 2 * EDGE * p + EDGE, 1)
+                acc = jnp.where(lane // (2 * EDGE) == p, x, acc)
             ek[f, pl.ds(y0, 8), :] = acc * scales[f]
         return 0
 
@@ -175,19 +175,19 @@
         copy.start()
         copies.append(copy)
 
-    def rows_of(start, size):
-        return yb.at[:, :, pl.ds(start, size)]
+    def rows_of(start):
+        return yb.at[pl.ds(0, 3), :, pl.ds(start, EDGE)]
+
+    def row_of(y):
+        return yb.at[pl.ds(3, 2), :, pl.ds(y, 1)]
 
     for copy in loads:
         copy.wait()
     for y in (*range(EDGE), *range(ny - EDGE, ny)):
         spread(y, 0)
-    pl.semaphore_wait(barrier, len(around))
-    remote(0, rows_of(EDGE, EDGE), rows_of(ny + EDGE, EDGE), (up, col))
-    remote(1, rows_of(ny, EDGE), rows_of(0, EDGE), (dn, col))
-
-    lax.fori_loop(0, ny // 8, pack, 0)
+    lax.fori_loop(0, ny // 8, pack, 0, unroll=2)
     fold = LANES // 32
+    slot = lane // 64 * 2 + lane // EDGE % 2
     part = ny // fold
     for f in range(5):
         for b in range(part // 8):
@@ -195,10 +195,15 @@
                 acc = None
                 for q in range(fold):
                     x = ek[f, pl.ds(q * part + b * 8, 8), :]
-                    turn = (32 * (q - side)) % LANES
+                    turn = (64 * (q // 2) + EDGE * (q % 2 - side)) % LANES
                     x = pltpu.roll(x, turn, 1) if turn else x
-                    acc = x if acc is None else jnp.where(lane // 32 == q, x, acc)
+                    acc = x if acc is None else jnp.where(slot == q, x, acc)
                 pk[side, f, pl.ds(b * 8, 8), :] = acc
+    pl.semaphore_wait(barrier, len(around))
+    remote(0, rows_of(EDGE), rows_of(ny + EDGE), (up, col))
+    remote(1, rows_of(ny), rows_of(0), (dn, col))
+    remote(8, row_of(EDGE), row_of(ny + EDGE), (up, col))
+    remote(9, row_of(ny + EDGE - 1), row_of(EDGE - 1), (dn, col))
     remote(2, pk.at[0], pr.at[0], (row, rt))
     remote(3, pk.at[1], pr.at[1], (row, lf))
     remote(4, ek.at[:, pl.ds(ny - 8, 8)], cr.at[0, 0], (dn, rt))
@@ -212,14 +217,14 @@
             return yb[f, h, i + EDGE]
 
         def cons():
-            r, x, y, z, p = (load(f, c - 3) for f in range(5))
+            r, y, p, x, z = (load(f, c - 3) for f in range(5))
             return conserved_of(r, y, x, z, p)
 
         def emit(*values):
             for f, x in enumerate(after_y_values(*values)):
                 ab[f, h, pl.ds(c - EDGE, planes, stride=ny), :] = x
 
-        return step(carry, tuple(load(f, c) for f in (0, 2, 4)), cons, emit)
+        return step(carry, tuple(load(f, c) for f in range(3)), cons, emit)
 
     def y_steps(carries, start, count):
         for k in range(count):
@@ -233,39 +238,41 @@
         lambda i, cr: y_steps(cr, 8 + i * UNROLL, UNROLL),
         carries,
     )
-    for copy in copies[:2]:
+    for copy in copies:
         copy.wait()
-    y_steps(carries, ny, EDGE)
-    y_steps((EMPTY,) * halves, -EDGE, 12)
-
-    for copy in copies[2:]:
-        copy.wait()
+
     for f in range(5):
         for end, start in ((0, 0), (1, ny + 8)):
-            hr[f, pl.ds(start, 8), :] = jnp.where(lane < 32, cr[0, end, f], cr[1, end, f])
+            hr[f, pl.ds(start, 8), :] = jnp.where(slot % 2 == 0, cr[0, end, f], cr[1, end, f])
         for b in range(part // 8):
             for q in range(fold):
                 x = [pr[side, f, pl.ds(b * 8, 8), :] for side in range(2)]
                 for side in range(2):
-                    turn = (32 * (side - q)) % LANES
+                    turn = (-64 * (q // 2) + EDGE * (side - q % 2)) % LANES
                     x[side] = pltpu.roll(x[side], turn, 1) if turn else x[side]
-                hr[f, pl.ds(8 + q * part + b * 8, 8), :] = jnp.where(lane < 32, *x)
+                hr[f, pl.ds(8 + q * part + b * 8, 8), :] = jnp.where(slot % 2 == 0, *x)
 
     def z_load(f, c):
         return hr[f, pl.ds(8 + c, 8, stride=ny // 8), :]
 
-    carry = EMPTY
-    for c in range(-EDGE, ny // 8 + EDGE):
-
-        def cons(c=c):
-            r, x, y, z, p = (z_load(f, c - 3) for f in range(5))
+    def z_edge(carry, c):
+        def cons():
+            r, y, p, x, z = (z_load(f, c - 3) for f in range(5))
             return conserved_of(r, y, x, z, p)
 
-        def emit(*values, c=c):
+        def emit(*values):
             for f, x in enumerate(after_y_values(*values)):
                 ho[f, pl.ds(c - EDGE, 8, stride=ny // 8), :] = x
 
-        carry = step(carry, tuple(z_load(f, c) for f in (0, 2, 4)), cons, emit)
+        return step(carry, tuple(z_load(f, c) for f in range(3)), cons, emit)
+
+    carry, first = EMPTY, (EMPTY,) * halves
+    for k in range(ny // 8 + 2 * EDGE):
+        carry = z_edge(carry, k - EDGE)
+        if k < 3 * EDGE:
+            first = y_steps(first, k - EDGE, 1)
+        if k < EDGE:
+            carries = y_steps(carries, ny + k, 1)
 
     pitch = LANES + 16
     groups = rows // LANES
@@ -280,12 +287,12 @@
                 if h + 1 < halves:
                     t_out[f, pl.ds(k + 8 + LANES, EDGE), :] = tiles[h + 1][:EDGE]
         edge = ho[f]
-        both = jnp.concatenate([edge, pltpu.roll(edge, LANES - EDGE, 1)], axis=0).T
+        both = jnp.concatenate([edge, pltpu.roll(edge, LANES - 2 * EDGE, 1)], axis=0).T
         for g in range(groups):
             k = g * halves * pitch
-            t_out[f, pl.ds(k + EDGE, EDGE), :] = both[8 * g : 8 * g + EDGE]
+            t_out[f, pl.ds(k + EDGE, EDGE), :] = both[16 * g : 16 * g + EDGE]
             k = (g * halves + halves - 1) * pitch
-            t_out[f, pl.ds(k + 8 + LANES, EDGE), :] = both[32 + 8 * g : 32 + 8 * g + EDGE]
+            t_out[f, pl.ds(k + 8 + LANES, EDGE), :] = both[16 * g + EDGE : 16 * g + 2 * EDGE]
 
 
 def z_kernel(planes, ny, halves, t_in, d_out, v_out, p_out, zb):
@@ -317,11 +324,11 @@
         carry = z_step(carry, c)
 
     def turn(i, carry):
-        for k in range(UNROLL):
-            carry = z_step(carry, EDGE + i * UNROLL + k)
+        for k in range(UNROLL_Z):
+            carry = z_step(carry, EDGE + i * UNROLL_Z + k)
         return carry
 
-    lax.fori_loop(0, LANES // UNROLL, turn, carry)
+    lax.fori_loop(0, LANES // UNROLL_Z, turn, carry)
 
     outs = [
         d_out,
@@ -362,8 +369,8 @@
             pltpu.VMEM((6, halves, rows, LANES), f32),
             pltpu.VMEM((6, ny, LANES), f32),
             pltpu.SemaphoreType.DMA((5, halves)),
-            pltpu.SemaphoreType.DMA((8,)),
-            pltpu.SemaphoreType.DMA((8,)),
+            pltpu.SemaphoreType.DMA((10,)),
+            pltpu.SemaphoreType.DMA((10,)),
         ],
         compiler_params=pltpu.CompilerParams(
             collective_id=0, has_side_effects=True, vmem_limit_bytes=40 * 2**20

time: 24.5 us -> 22.2 us (0.906)
  Pallas kernels: 23.7 us -> 21.4 us
    pallas_call x1, Pallas kernels: 17.4 us -> 15.8 us  [on_device(): pl.pallas_call(functools.partial(y_kernel, axes, planes, ny, halves), out...]
    pallas_call x1, Pallas kernels: 6.34 us -> 5.66 us  [on_device(): pl.pallas_call(functools.partial(z_kernel, planes, ny, halves), out_shape...]
where the time goes in v2:
time: 22.2 us; the launch traced here: 22.1 us
  Pallas kernels  21.4 us (96%)
  between operations  0.64 us (3%)
    pallas_call x1, Pallas kernels, on_device(): pl.pallas_call(functools.partial(y_kernel, axes, planes, ny, halves), out...  15.8 us
    pallas_call x1, Pallas kernels, on_device(): pl.pallas_call(functools.partial(z_kernel, planes, ny, halves), out_shape...  5.66 us

profile of v2, /device:TPU:0, one launch (start us, length us, event | category | flops | bytes accessed | tf_op | source)
XLA Modules:
  0.0 22.1 jit_solution(1216380468232877335)
XLA Ops:
  0.6 15.8 %shard_map.58.t_in = f32[6,1152,128]{2,1,0:T(8,128)S(1)} custom-call(f32[512,256]{1,0:T(8,128)} %bitcast.7, f32[1536,256]{1,0:T(8,128)} %bitcast.6, f32[512,256]{1,0:T(8,128)} %bitcast.8), custom_call_target="tpu_custom_call" | custom-call | tf_op jit(solution)/shard_map/pallas_call | solution.py:356
  16.4 5.7 %shard_map.59 = (f32[512,256]{1,0:T(8,128)}, f32[1536,256]{1,0:T(8,128)}, f32[512,256]{1,0:T(8,128)}) custom-call(f32[6,1152,128]{2,1,0:T(8,128)S(1)} %shard_map.58.t_in), custom_call_target="tpu_custom_call" | custom-call | tf_op jit(solution)/shard_map/pallas_call | solution.py:384
